TPU v7x, 512 devices: a whole 4x8x8 slice. The times are simulated.
512 devices in a mesh: seq: 32 (over y, x), head: 16 (over z, core).
Axes of the slice: x: 4, y: 8, z: 8, core: 2. Of those that a mesh axis runs over, the one named last changes fastest.
Arguments:
- queries: bfloat16 [65536, 4096], P(('seq', 'head')), may hold values from -2.59375 to 2.59375
- key_matrix: bfloat16 [65536, 512], P(('seq', 'head')), may hold values from -2.59375 to 2.59375
- value_matrix: bfloat16 [65536, 512], P(('seq', 'head')), may hold values from -6 to 6
- attn_output: bfloat16 [65536, 4096], P(('seq', 'head')), may hold values from -6 to 6
- grad_output: bfloat16 [65536, 4096], P(('seq', 'head')), may hold values from -6 to 6
- prefix_len: int32 [32], replicated, may hold values from 1 to 128, as said below
- rollout_len: int32 [32, 15], replicated, may hold values from 1 to 128, as said below
- rollout_prompt: int32 [480, 1], replicated, may hold values from 0 to 31
- prefix_owner: int32 [32], replicated, may hold values from 0 to 31, each once
Outputs:
- grad_query: bfloat16 [65536, 4096], P(('seq', 'head'))
- key_gradient: bfloat16 [65536, 512], P(('seq', 'head'))
- value_gradient: bfloat16 [65536, 512], P(('seq', 'head'))
Inputs may be any that keep to these rules, and one draw needn't show every extreme that they name: `prefix_len`: some prompt's prefix is live in all 128 rows. `rollout_len`: some slot is live in all 128 rows. `rollout_prompt`: every prompt has at least one rollout slot. `prefix_owner`: each shard stores exactly one prefix.
All inputs are finite; a program needn't handle non-finite values.
Results may differ from a plain program's by a relative error of at most 0.0054.
Values may be sent and summed in bfloat16 or wider, within the bound.
A program may use at most 64 MiB of HBM per device.

v0:
```python
import math

import jax
import jax.numpy as jnp
import numpy as np
from jax import lax
from jax.sharding import PartitionSpec as P

QUERY_HEADS = 32
KEY_VALUE_HEADS = 4
HEAD_SIZE = 128
PREFIX_ROWS = 128
RLEN = 128


def attend(query_rows, grad_rows, delta_rows, key_rows, value_rows, allowed):
    factor = 1.0 / math.sqrt(HEAD_SIZE)
    scores = (
        jnp.einsum("rhd,khd->hrk", query_rows, key_rows, preferred_element_type=jnp.float32)
        * factor
    )
    raised = jnp.where(allowed[None], jnp.exp(scores), 0.0)
    row_total = jnp.sum(raised, axis=-1, keepdims=True)
    live_rows = jnp.any(allowed, axis=-1)[None, :, None]
    weights = raised / jnp.where(live_rows, row_total, 1.0)
    weights_low = weights.astype(jnp.bfloat16)
    value_gradient = jnp.einsum(
        "hrk,rhd->khd", weights_low, grad_rows, preferred_element_type=jnp.float32
    )
    grad_weights = jnp.einsum(
        "rhd,khd->hrk", grad_rows, value_rows, preferred_element_type=jnp.float32
    )
    grad_scores = weights * (grad_weights - jnp.transpose(delta_rows)[:, :, None])
    scores_low = grad_scores.astype(jnp.bfloat16)
    grad_query = (
        jnp.einsum("hrk,khd->rhd", scores_low, key_rows, preferred_element_type=jnp.float32)
        * factor
    )
    key_gradient = (
        jnp.einsum("hrk,rhd->khd", scores_low, query_rows, preferred_element_type=jnp.float32)
        * factor
    )
    return (grad_query, key_gradient, value_gradient)


def prefix_mask(live_count):
    positions = jnp.arange(PREFIX_ROWS, dtype=jnp.int32)
    return (positions[None, :] <= positions[:, None]) & (positions[:, None] < live_count)


def slot_mask(prefix_count, live_count):
    rows_here = jnp.arange(RLEN, dtype=jnp.int32)
    columns = jnp.arange(PREFIX_ROWS, dtype=jnp.int32)
    live_rows = rows_here < live_count
    remote = live_rows[:, None] & (columns[None, :] < prefix_count)
    local = live_rows[:, None] & (rows_here[None, :] <= rows_here[:, None])
    return jnp.concatenate([remote, local], axis=1)


def group_sum(values, key_value_heads):
    shape = values.shape
    return jnp.sum(
        values.reshape(shape[:-2] + (key_value_heads, shape[-2] // key_value_heads, shape[-1])),
        axis=-2,
    )


def shards(
    queries,
    key_matrix,
    value_matrix,
    attn_output,
    grad_output,
    prefix_len,
    rollout_len,
    rollout_prompt,
    prefix_owner,
):
    count_of_heads = lax.axis_size("head")
    seq_count = lax.axis_size("seq")
    my_shard = lax.axis_index("seq")
    token_rows = queries.shape[0]
    group_heads = QUERY_HEADS // count_of_heads
    key_value_heads = max(1, KEY_VALUE_HEADS // count_of_heads)
    group_width = QUERY_HEADS // KEY_VALUE_HEADS
    shard_rows = token_rows * count_of_heads
    slot_count = rollout_len.shape[1]
    products = grad_output.reshape(token_rows, QUERY_HEADS, HEAD_SIZE).astype(
        jnp.float32
    ) * attn_output.reshape(token_rows, QUERY_HEADS, HEAD_SIZE).astype(jnp.float32)
    deltas = (
        jnp.sum(products, axis=-1)
        .astype(jnp.bfloat16)
        .reshape(token_rows, count_of_heads, group_heads)
    )
    query_slots = queries.reshape(token_rows, count_of_heads, group_heads * HEAD_SIZE)
    grad_slots = grad_output.reshape(token_rows, count_of_heads, group_heads * HEAD_SIZE)
    heads_of_keys = key_matrix.reshape(token_rows, KEY_VALUE_HEADS, HEAD_SIZE)
    heads_of_values = value_matrix.reshape(token_rows, KEY_VALUE_HEADS, HEAD_SIZE)
    remote_index = np.arange(group_heads) // (group_heads // key_value_heads)
    outbound_index = np.arange(QUERY_HEADS) // group_width
    expand_index = np.arange(group_heads)
    pick_index = np.arange(key_value_heads) * (group_heads // key_value_heads)
    summation_table = np.eye(KEY_VALUE_HEADS, dtype=np.float32)[outbound_index]
    key_slots = jnp.take(heads_of_keys, outbound_index, axis=1).reshape(
        token_rows, count_of_heads, group_heads * HEAD_SIZE
    )
    value_slots = jnp.take(heads_of_values, outbound_index, axis=1).reshape(
        token_rows, count_of_heads, group_heads * HEAD_SIZE
    )
    got_query, got_grad, got_delta, got_key, got_value = (
        lax.all_to_all(query_slots, "head", split_axis=1, concat_axis=0, tiled=True),
        lax.all_to_all(grad_slots, "head", split_axis=1, concat_axis=0, tiled=True),
        lax.all_to_all(deltas, "head", split_axis=1, concat_axis=0, tiled=True),
        lax.all_to_all(key_slots, "head", split_axis=1, concat_axis=0, tiled=True),
        lax.all_to_all(value_slots, "head", split_axis=1, concat_axis=0, tiled=True),
    )
    query_rows = got_query.reshape(shard_rows, group_heads, HEAD_SIZE)
    grad_rows = got_grad.reshape(shard_rows, group_heads, HEAD_SIZE)
    delta_rows = got_delta.reshape(shard_rows, group_heads).astype(jnp.float32)
    key_rows = got_key.reshape(shard_rows, group_heads, HEAD_SIZE)
    value_rows = got_value.reshape(shard_rows, group_heads, HEAD_SIZE)
    key_expanded = jnp.take(key_rows, expand_index, axis=1)
    value_expanded = jnp.take(value_rows, expand_index, axis=1)
    own_key = jnp.take(key_rows[:PREFIX_ROWS], pick_index, axis=1).reshape(
        1, PREFIX_ROWS, key_value_heads * HEAD_SIZE
    )
    own_value = jnp.take(value_rows[:PREFIX_ROWS], pick_index, axis=1).reshape(
        1, PREFIX_ROWS, key_value_heads * HEAD_SIZE
    )
    all_keys, all_values = (
        lax.all_gather(own_key, "seq", axis=0, tiled=True),
        lax.all_gather(own_value, "seq", axis=0, tiled=True),
    )
    own_len = jnp.sum(jnp.where(prefix_owner == my_shard, prefix_len, 0))
    pre_query, pre_key, pre_value = attend(
        query_rows[:PREFIX_ROWS],
        grad_rows[:PREFIX_ROWS],
        delta_rows[:PREFIX_ROWS],
        key_expanded[:PREFIX_ROWS],
        value_expanded[:PREFIX_ROWS],
        prefix_mask(own_len),
    )
    prompts = lax.dynamic_slice_in_dim(rollout_prompt[:, 0], my_shard * slot_count, slot_count)
    live_lens = lax.dynamic_index_in_dim(rollout_len, my_shard, 0, keepdims=False)
    sources = prefix_owner[prompts]
    prefix_counts = prefix_len[prompts]
    remote_keys = jnp.take(
        jnp.take(
            all_keys.reshape(seq_count, PREFIX_ROWS, key_value_heads, HEAD_SIZE), sources, axis=0
        ),
        remote_index,
        axis=2,
    )
    remote_values = jnp.take(
        jnp.take(
            all_values.reshape(seq_count, PREFIX_ROWS, key_value_heads, HEAD_SIZE), sources, axis=0
        ),
        remote_index,
        axis=2,
    )

    def slot_view(array):
        return array[PREFIX_ROWS:].reshape((slot_count, RLEN) + array.shape[1:])

    def one_slot(items):
        (
            slot_query,
            slot_grad,
            slot_delta,
            slot_key,
            slot_value,
            distant_key,
            distant_value,
            prefix_count,
            live_count,
        ) = items
        allowed = slot_mask(prefix_count, live_count)
        out_query, out_key, out_value = attend(
            slot_query,
            slot_grad,
            slot_delta,
            jnp.concatenate([distant_key, slot_key], axis=0),
            jnp.concatenate([distant_value, slot_value], axis=0),
            allowed,
        )
        return (
            out_query,
            out_key[PREFIX_ROWS:],
            out_value[PREFIX_ROWS:],
            group_sum(out_key[:PREFIX_ROWS], key_value_heads),
            group_sum(out_value[:PREFIX_ROWS], key_value_heads),
        )

    slot_items = (
        slot_view(query_rows),
        slot_view(grad_rows),
        slot_view(delta_rows),
        slot_view(key_expanded),
        slot_view(value_expanded),
        remote_keys,
        remote_values,
        prefix_counts,
        live_lens,
    )
    slot_query, slot_key, slot_value, distant_key, distant_value = lax.map(one_slot, slot_items)
    local_key = jnp.concatenate(
        [pre_key, slot_key.reshape(slot_count * RLEN, group_heads, HEAD_SIZE)], axis=0
    )
    local_value = jnp.concatenate(
        [pre_value, slot_value.reshape(slot_count * RLEN, group_heads, HEAD_SIZE)], axis=0
    )
    owning_shards = (sources[:, None] == jnp.arange(seq_count, dtype=jnp.int32)[None, :]).astype(
        jnp.float32
    )
    bucket_key = jnp.einsum(
        "iq,iz->qz",
        owning_shards,
        distant_key.reshape(slot_count, -1),
        precision=lax.Precision.HIGHEST,
    ).reshape(seq_count, PREFIX_ROWS, key_value_heads * HEAD_SIZE)
    bucket_value = jnp.einsum(
        "iq,iz->qz",
        owning_shards,
        distant_value.reshape(slot_count, -1),
        precision=lax.Precision.HIGHEST,
    ).reshape(seq_count, PREFIX_ROWS, key_value_heads * HEAD_SIZE)
    back_key, back_value = (
        lax.psum_scatter(bucket_key, "seq", scatter_dimension=0, tiled=True),
        lax.psum_scatter(bucket_value, "seq", scatter_dimension=0, tiled=True),
    )
    local_key = local_key.at[:PREFIX_ROWS, pick_index].add(
        back_key.reshape(PREFIX_ROWS, key_value_heads, HEAD_SIZE)
    )
    local_value = local_value.at[:PREFIX_ROWS, pick_index].add(
        back_value.reshape(PREFIX_ROWS, key_value_heads, HEAD_SIZE)
    )
    query_grads = jnp.concatenate(
        [pre_query, slot_query.reshape(slot_count * RLEN, group_heads, HEAD_SIZE)], axis=0
    ).astype(jnp.bfloat16)
    returned_query = lax.all_to_all(
        query_grads.reshape(shard_rows, 1, group_heads * HEAD_SIZE),
        "head",
        split_axis=0,
        concat_axis=1,
        tiled=True,
    )
    sent_key = local_key.reshape(shard_rows, 1, group_heads * HEAD_SIZE)
    sent_value = local_value.reshape(shard_rows, 1, group_heads * HEAD_SIZE)
    returned_key, returned_value = (
        lax.all_to_all(sent_key, "head", split_axis=0, concat_axis=1, tiled=True),
        lax.all_to_all(sent_value, "head", split_axis=0, concat_axis=1, tiled=True),
    )
    key_gradient = jnp.einsum(
        "tsd,sk->tkd",
        returned_key.reshape(token_rows, count_of_heads * group_heads, HEAD_SIZE),
        summation_table,
        precision=lax.Precision.HIGHEST,
    )
    value_gradient = jnp.einsum(
        "tsd,sk->tkd",
        returned_value.reshape(token_rows, count_of_heads * group_heads, HEAD_SIZE),
        summation_table,
        precision=lax.Precision.HIGHEST,
    )
    return (
        returned_query.reshape(token_rows, QUERY_HEADS * HEAD_SIZE),
        key_gradient.astype(jnp.bfloat16).reshape(token_rows, KEY_VALUE_HEADS * HEAD_SIZE),
        value_gradient.astype(jnp.bfloat16).reshape(token_rows, KEY_VALUE_HEADS * HEAD_SIZE),
    )


def solution(mesh):
    in_specs = (
        P(("seq", "head"), None),
        P(("seq", "head"), None),
        P(("seq", "head"), None),
        P(("seq", "head"), None),
        P(("seq", "head"), None),
        P(),
        P(),
        P(),
        P(),
    )
    out_specs = (P(("seq", "head"), None), P(("seq", "head"), None), P(("seq", "head"), None))
    return jax.shard_map(shards, mesh=mesh, in_specs=in_specs, out_specs=out_specs, check_vma=False)
```

profile of v0, /device:TPU:1, one launch (start us, length us, event | category | flops | bytes accessed | tf_op | source)
XLA Modules:
  0.0 957.5 jit_solution(9633377713572545905)
XLA Ops:
  7.2 1.8 multiply_bitcast_fusion
  10.7 11.8 %all-to-all-start.4 = ((bf16[128,16,2]{0,2,1:T(2,128)(2,1)}), bf16[128,16,2]{0,2,1:T(2,128)(2,1)S(1)}, u32[]{:S(2)}, u32[]{:S(2)}) async-start(bf16[128,16,2]{0,2,1:T(2,128)(2,1)} %bitcast.39), calls=%async_computation.4 | async-start | bytes 16384 | tf_op jit(solution)/shard_map/all_to_all | solution.py:114
  24.9 4.6 all-to-all-done.4
  29.5 4.1 all-to-all-start.2
  36.0 25.6 %all-to-all-done.2 = bf16[128,16,256]{0,2,1:T(8,128)(2,1)S(1)} async-done(((bf16[128,16,256]{0,2,1:T(8,128)(2,1)}), bf16[128,16,256]{0,2,1:T(8,128)(2,1)S(1)}, u32[]{:S(2)}, u32[]{:S(2)}) %all-to-all-start.2) | async-done | bytes 1048608 | tf_op jit(solution)/shard_map/all_to_all | solution.py:116
  61.6 3.6 all-to-all-start
  67.2 25.8 %all-to-all-done = bf16[128,16,256]{0,2,1:T(8,128)(2,1)S(1)} async-done(((bf16[128,16,256]{0,2,1:T(8,128)(2,1)}), bf16[128,16,256]{0,2,1:T(8,128)(2,1)S(1)}, u32[]{:S(2)}, u32[]{:S(2)}) %all-to-all-start) | async-done | bytes 1048608 | tf_op jit(solution)/shard_map/all_to_all | solution.py:115
  93.0 3.6 all-to-all-start.1
  97.4 2.3 copy.230
  99.7 24.8 %all-to-all-done.1 = bf16[128,16,256]{0,2,1:T(8,128)(2,1)S(1)} async-done(((bf16[128,16,256]{0,2,1:T(8,128)(2,1)}), bf16[128,16,256]{0,2,1:T(8,128)(2,1)S(1)}, u32[]{:S(2)}, u32[]{:S(2)}) %all-to-all-start.1) | async-done | bytes 1048608 | tf_op jit(solution)/shard_map/all_to_all | solution.py:112
  124.5 4.2 all-to-all-start.3
  144.6 11.5 %all-to-all-done.3 = bf16[128,16,256]{0,2,1:T(8,128)(2,1)} async-done(((bf16[128,16,256]{0,2,1:T(8,128)(2,1)}), bf16[128,16,256]{0,2,1:T(8,128)(2,1)}, u32[]{:S(2)}, u32[]{:S(2)}) %all-to-all-start.3) | async-done | bytes 1048608 | tf_op jit(solution)/shard_map/all_to_all | solution.py:113
  156.0 2.3 slice.179
  160.6 61.2 %all-gather.5.cloned.1.call-done = bf16[4096,1,128]{0,2,1:T(8,128)(2,1)} async-done(((bf16[128,1,128]{0,2,1:T(8,128)(2,1)}), bf16[4096,1,128]{0,2,1:T(8,128)(2,1)}) %all-gather.5.cloned.1.call-update) | async-done | bytes 1048592 | tf_op jit(solution)/shard_map/all_gather | solution.py:132
  225.7 191.0 %while.21 = (s32[]{:T(128)}, bf16[15,128,2,128]{1,3,2,0:T(8,128)(2,1)}, f32[15,128,2,128]{3,1,0,2:T(8,128)}, f32[15,128,2,128]{3,1,0,2:T(8,128)}, f32[15,128,1,1...) while((s32[]{:T(128)}, ...), condition=%wide.region_10.16_spmd, body=%wide.region_4.15_spmd.sunk | while | flops 85508224 | bytes 5645805 | solution.py:206
  419.5 1.9 copy.259
  431.9 12.3 %all-to-all-start.5 = ((bf16[16,2,16384]{2,1,0:T(2,128)(2,1)}), bf16[16,2,16384]{2,1,0:T(2,128)(2,1)S(1)}, u32[]{:S(2)}, u32[]{:S(2)}) async-start(bf16[16,2,16384]{2,1,0:T(2,128)(2,1)} %reshape.560), calls=%async_computation.5 | async-start | bytes 2097152 | tf_op jit(solution)/shard_map/all_to_all | solution.py:241
  446.4 2.5 copy.250
  450.7 190.8 %reduce-scatter.5.cloned.1.call-done = f32[1,128,128]{1,2,0:T(8,128)} async-done(((f32[32,128,128]{1,2,0:T(8,128)}), f32[1,128,128]{1,2,0:T(8,128)}) %reduce-scatter.5.cloned.1.call-update) | async-done | bytes 65552 | tf_op jit(solution)/shard_map/reduce_scatter | solution.py:230
  642.5 1.8 copy.261
  644.3 6.0 copy.262
  650.3 13.0 %all-to-all-start.7 = ((f32[2048,1,256]{2,1,0:T(1,128)}), f32[2048,1,256]{2,1,0:T(1,128)S(1)}, u32[]{:S(2)}, u32[]{:S(2)}) async-start(f32[2048,1,256]{2,1,0:T(1,128)} %copy.262), calls=%async_computation.9 | async-start | bytes 4194304 | tf_op jit(solution)/shard_map/all_to_all | solution.py:252
  663.6 3.0 pad_maximum_fusion.3
  666.6 200.0 %reduce-scatter.3.cloned.1.call-done = f32[1,128,128]{2,1,0:T(8,128)} async-done(((f32[32,128,128]{2,1,0:T(8,128)}), f32[1,128,128]{2,1,0:T(8,128)}) %reduce-scatter.3.cloned.1.call-update) | async-done | bytes 65552 | tf_op jit(solution)/shard_map/reduce_scatter | solution.py:229
  868.1 3.0 copy.251
  871.1 6.0 copy.252
  878.4 13.0 %all-to-all-start.6 = ((f32[2048,1,256]{2,1,0:T(1,128)}), f32[2048,1,256]{2,1,0:T(1,128)}, u32[]{:S(2)}, u32[]{:S(2)}) async-start(f32[2048,1,256]{2,1,0:T(1,128)} %copy.252), calls=%async_computation.7 | async-start | bytes 4194304 | tf_op jit(solution)/shard_map/all_to_all | solution.py:251
  894.1 2.3 copy.264
  896.5 2.6 copy.263
  900.7 39.9 %all-to-all-done.6 = f32[2048,1,256]{2,1,0:T(1,128)} async-done(((f32[2048,1,256]{2,1,0:T(1,128)}), f32[2048,1,256]{2,1,0:T(1,128)}, u32[]{:S(2)}, u32[]{:S(2)}) %all-to-all-start.6) | async-done | bytes 2097184 | tf_op jit(solution)/shard_map/all_to_all | solution.py:251
  942.2 2.5 copy.253
  944.8 2.6 reshape.394
  (516 shorter events, 250.8 us)
Async XLA Ops:
  7.2 123.9 %copy-start = (s32[32,15]{0,1:T(8,128)S(1)}, s32[32,15]{0,1:T(8,128)}, u32[]{:S(2)}) copy-start(s32[32,15]{0,1:T(8,128)} %param.39) | copy-start | bytes 5764
  9.4 13.2 %copy-start.16 = (s32[32]{0:T(128)S(1)}, s32[32]{0:T(128)}, u32[]{:S(2)}) copy-start(s32[32]{0:T(128)} %constant.246) | copy-start | bytes 388
  9.4 13.2 %copy-start.13 = (bf16[128,512]{1,0:T(8,128)(2,1)S(1)}, bf16[128,512]{1,0:T(8,128)(2,1)}, u32[]{:S(2)}) copy-start(bf16[128,512]{1,0:T(8,128)(2,1)} %param.35) | copy-start | bytes 393220
  10.7 18.8 %all-to-all-start.4 = ((bf16[128,16,2]{0,2,1:T(2,128)(2,1)}), bf16[128,16,2]{0,2,1:T(2,128)(2,1)S(1)}, u32[]{:S(2)}, u32[]{:S(2)}) async-start(bf16[128,16,2]{0,2,1:T(2,128)(2,1)} %bitcast.39), calls=%async_computation.4 | async-start | bytes 16384 | tf_op jit(solution)/shard_map/all_to_all | solution.py:114
  23.6 10.0 %copy-start.14 = (bf16[128,512]{1,0:T(8,128)(2,1)S(1)}, bf16[128,512]{1,0:T(8,128)(2,1)}, u32[]{:S(2)}) copy-start(bf16[128,512]{1,0:T(8,128)(2,1)} %param.34) | copy-start | bytes 393220
  29.5 32.1 %all-to-all-start.2 = ((bf16[128,16,256]{0,2,1:T(8,128)(2,1)}), bf16[128,16,256]{0,2,1:T(8,128)(2,1)S(1)}, u32[]{:S(2)}, u32[]{:S(2)}) async-start(bf16[128,16,256]{0,2,1:T(8,128)(2,1)} %bitcast.31), calls=%async_computation.2 | async-start | bytes 2097152 | tf_op jit(solution)/shard_map/all_to_all | solution.py:116
  34.6 31.2 %copy-start.10 = (bf16[128,4096]{1,0:T(8,128)(2,1)S(1)}, bf16[128,4096]{1,0:T(8,128)(2,1)}, u32[]{:S(2)}) copy-start(bf16[128,4096]{1,0:T(8,128)(2,1)} %param.33) | copy-start | bytes 3145732
  61.6 31.5 %all-to-all-start = ((bf16[128,16,256]{0,2,1:T(8,128)(2,1)}), bf16[128,16,256]{0,2,1:T(8,128)(2,1)S(1)}, u32[]{:S(2)}, u32[]{:S(2)}) async-start(bf16[128,16,256]{0,2,1:T(8,128)(2,1)} %bitcast.20), calls=%async_computation | async-start | bytes 2097152 | tf_op jit(solution)/shard_map/all_to_all | solution.py:115
  65.1 93.3 %all-gather.7.cloned.1.call-start = ((), (), s32[]{:S(2)}) async-start(), calls=%async_computation.13 | async-start | bytes 1081344 | tf_op jit(solution)/shard_map/all_gather | solution.py:133
  93.0 31.5 %all-to-all-start.1 = ((bf16[128,16,256]{0,2,1:T(8,128)(2,1)}), bf16[128,16,256]{0,2,1:T(8,128)(2,1)S(1)}, u32[]{:S(2)}, u32[]{:S(2)}) async-start(bf16[128,16,256]{0,2,1:T(8,128)(2,1)} %bitcast.270), calls=%async_computation.1 | async-start | bytes 2097152 | tf_op jit(solution)/shard_map/all_to_all | solution.py:112
  96.6 125.2 %all-gather.5.cloned.1.call-start = ((), (), s32[]{:S(2)}) async-start(), calls=%async_computation.12 | async-start | bytes 1081344 | tf_op jit(solution)/shard_map/all_gather | solution.py:132
  97.4 32.4 %copy-start.2 = (s32[32]{0:T(128)S(1)}, s32[32]{0:T(128)}, u32[]{:S(2)}) copy-start(s32[32]{0:T(128)} %param.41) | copy-start | bytes 388
  97.4 33.0 %copy-start.3 = (s32[32]{0:T(128)S(1)}, s32[32]{0:T(128)}, u32[]{:S(2)}) copy-start(s32[32]{0:T(128)} %param.38) | copy-start | bytes 388
  124.5 8.5 copy-start.7
  124.5 31.6 %all-to-all-start.3 = ((bf16[128,16,256]{0,2,1:T(8,128)(2,1)}), bf16[128,16,256]{0,2,1:T(8,128)(2,1)}, u32[]{:S(2)}, u32[]{:S(2)}) async-start(bf16[128,16,256]{0,2,1:T(8,128)(2,1)} %bitcast.269), calls=%async_computation.3 | async-start | bytes 2097152 | tf_op jit(solution)/shard_map/all_to_all | solution.py:113
  128.7 512.8 %reduce-scatter.5.cloned.1.call-start = ((), (), s32[]{:S(2)}) async-start(), calls=%async_computation.11 | async-start | bytes 2162688 | tf_op jit(solution)/shard_map/reduce_scatter | solution.py:230
  140.6 1.0 copy-start.9
  140.6 3.0 copy-start.8
  421.3 5.2 copy-start.12
  424.6 0.7 copy-start.17
  430.8 14.0 %copy-start.11 = (f32[15,128,1,128]{3,1,0,2:T(8,128)S(1)}, f32[15,128,1,128]{3,1,0,2:T(8,128)}, u32[]{:S(2)}) copy-start(f32[15,128,1,128]{3,1,0,2:T(8,128)} %get-tuple-element.115) | copy-start | bytes 2949124
  431.9 12.6 %copy-start.18 = (f32[2,128,128]{1,2,0:T(8,128)S(1)}, f32[2,128,128]{1,2,0:T(8,128)}, u32[]{:S(2)}) copy-start(f32[2,128,128]{1,2,0:T(8,128)} %copy-done.17) | copy-start | bytes 393220
  431.9 218.4 %all-to-all-start.5 = ((bf16[16,2,16384]{2,1,0:T(2,128)(2,1)}), bf16[16,2,16384]{2,1,0:T(2,128)(2,1)S(1)}, u32[]{:S(2)}, u32[]{:S(2)}) async-start(bf16[16,2,16384]{2,1,0:T(2,128)(2,1)} %reshape.560), calls=%async_computation.5 | async-start | bytes 2097152 | tf_op jit(solution)/shard_map/all_to_all | solution.py:241
  444.2 422.4 %reduce-scatter.3.cloned.1.call-start = ((), (), s32[]{:S(2)}) async-start(), calls=%async_computation.10 | async-start | bytes 2162688 | tf_op jit(solution)/shard_map/reduce_scatter | solution.py:229
  650.3 226.8 %all-to-all-start.7 = ((f32[2048,1,256]{2,1,0:T(1,128)}), f32[2048,1,256]{2,1,0:T(1,128)S(1)}, u32[]{:S(2)}, u32[]{:S(2)}) async-start(f32[2048,1,256]{2,1,0:T(1,128)} %copy.262), calls=%async_computation.9 | async-start | bytes 4194304 | tf_op jit(solution)/shard_map/all_to_all | solution.py:252
  877.1 1.3 copy-start.5
  878.4 62.1 %all-to-all-start.6 = ((f32[2048,1,256]{2,1,0:T(1,128)}), f32[2048,1,256]{2,1,0:T(1,128)}, u32[]{:S(2)}, u32[]{:S(2)}) async-start(f32[2048,1,256]{2,1,0:T(1,128)} %copy.252), calls=%async_computation.7 | async-start | bytes 4194304 | tf_op jit(solution)/shard_map/all_to_all | solution.py:251
  892.7 3.6 copy-start.6
  944.8 2.6 copy-start.15
  944.8 6.2 copy-start.1
  947.4 1.6 copy-start.4
Sparse Core Ops, SparseCore 0:
  69.6 73.2 all-gather.6
  146.5 75.2 all-gather.4
  421.5 219.9 reduce-scatter.4
  646.4 220.1 reduce-scatter.2
where the time goes:
time: 964 us; the launch traced here: 958 us
  waiting for transfers between devices  584 us (61%)
  local copies, waits for them, and re-layouts  169 us (18%)
  matrix products  85.5 us (9%)
  starting transfers between devices  66.2 us (7%)
  other arithmetic  36.6 us (4%)
  between operations  14.4 us (1%)
    reduce_scatter x1, waiting for transfers between devices, shards(): lax.psum_scatter(bucket_key, 'seq', scatter_dimension=0, tiled=True)  200 us
    reduce_scatter x1, waiting for transfers between devices, shards(): lax.psum_scatter(bucket_value, 'seq', scatter_dimension=0, tiled=True)  191 us
    all_gather x1, waiting for transfers between devices, shards(): lax.all_gather(own_key, 'seq', axis=0, tiled=True)  61.2 us
    dynamic_update_slice x120, local copies, waits for them, and re-layouts, shards(): lax.map(one_slot, slot_items)  43.9 us
    all_to_all x1, waiting for transfers between devices, shards(): lax.all_to_all(sent_key, 'head', split_axis=0, concat_axis=1, tiled=True)  39.9 us
    squeeze x30, local copies, waits for them, and re-layouts, shards(): lax.map(one_slot, slot_items)  26.3 us
    all_to_all x1, waiting for transfers between devices, shards(): lax.all_to_all(key_slots, 'head', split_axis=1, concat_axis=0, tiled=True)  25.8 us
    all_to_all x1, waiting for transfers between devices, shards(): lax.all_to_all(value_slots, 'head', split_axis=1, concat_axis=0, tiled=True)  25.6 us
  transfers between devices with their start and end apart: 12, of which 9 were waited for; matrix products, arithmetic and copies ran while one was open for 8% of the time, Pallas kernels for 0%

commit v1 on v0

v1 whole, which is shorter than its diff:
```python
import functools
import math

import jax
import jax.numpy as jnp
from jax import lax
from jax.experimental import pallas as pl
from jax.experimental.pallas import tpu as pltpu
from jax.sharding import PartitionSpec as P

QUERY_HEADS = 32
KEY_VALUE_HEADS = 4
HEAD_SIZE = 128
PREFIX_ROWS = 128
RLEN = 128
MESH = pl.DeviceIdType.MESH
F32 = jnp.float32
BF16 = jnp.bfloat16
VMEM_BYTES = 60 * 1024 * 1024


def mm(a, b, da, db):
    return lax.dot_general(a, b, (((da,), (db,)), ((), ())), preferred_element_type=F32)


def kernel(
    ny,
    nx,
    nt,
    prompt_ref,
    owner_ref,
    plen_ref,
    rlen_ref,
    q_hbm,
    k_hbm,
    v_hbm,
    o_hbm,
    do_hbm,
    dq_hbm,
    dk_hbm,
    dv_hbm,
    q,
    k,
    v,
    o,
    do,
    dq,
    dk,
    dv,
    strip,
    units,
    picked,
    pre,
    back_out,
    back,
    sums,
    parts,
    final,
    spread,
    exps,
    prods,
    ds_pre,
    w_low,
    ds_low,
    delta,
    total,
    in_sem,
    out_sem,
    send_sem,
    recv_sem,
):
    n_seq = ny * nx
    group = nx * nt
    heads = q.shape[1] // (nx * HEAD_SIZE)
    unit_rows = PREFIX_ROWS // (nt // 2)
    width = heads * HEAD_SIZE
    factor = 1.0 / math.sqrt(HEAD_SIZE)
    s = lax.axis_index("seq")
    t = lax.axis_index("head")
    y = s // nx
    x = s % nx
    kind = t % 2
    block = t // 2

    def each(count, body, start=0):
        def step(i, carry):
            body(i)
            return carry

        lax.fori_loop(start, count, step, 0)

    loads = [
        pltpu.make_async_copy(a, b, in_sem.at[i])
        for i, (a, b) in enumerate(((q_hbm, q), (k_hbm, k), (v_hbm, v), (do_hbm, do), (o_hbm, o)))
    ]
    for load in loads:
        load.start()

    barrier = pltpu.get_barrier_semaphore()

    def greet_row(i):
        peer = (y * nx + (x + i // nt) % nx, (t + i) % nt)
        pl.semaphore_signal(barrier, inc=1, device_id=peer, device_id_type=MESH)

    def greet_plane(i):
        peer = (((y + 1 + i // nx) % ny) * nx + i % nx, t)
        pl.semaphore_signal(barrier, inc=1, device_id=peer, device_id_type=MESH)

    each(group, greet_row, 1)
    each((ny - 1) * nx, greet_plane)
    pl.semaphore_wait(barrier, group - 1 + (ny - 1) * nx)

    def remote(src, dst, stage, peer):
        return pltpu.make_async_remote_copy(
            src_ref=src,
            dst_ref=dst,
            send_sem=send_sem.at[stage],
            recv_sem=recv_sem.at[stage],
            device_id=peer,
            device_id_type=MESH,
        )

    def local(src, dst, stage):
        return pltpu.make_async_copy(src, dst, recv_sem.at[stage])

    def arrived(ref, stage):
        pltpu.make_async_copy(ref, ref, recv_sem.at[stage]).wait()

    def sent(ref, stage):
        pltpu.make_async_copy(ref, ref, send_sem.at[stage]).wait()

    @pl.when(t == 0)
    def _():
        local(k_hbm.at[pl.ds(0, unit_rows)], strip, 0).start()
        remote(v_hbm.at[pl.ds(0, unit_rows)], strip, 0, (s, 1)).start()

        def send_strips(i):
            rows = pl.ds(pl.multiple_of(i * unit_rows, unit_rows), unit_rows)
            remote(k_hbm.at[rows], strip, 0, (s, 2 * i)).start()
            remote(v_hbm.at[rows], strip, 0, (s, 2 * i + 1)).start()

        each(nt // 2, send_strips, 1)

    def source(x2, t2):
        at = (y * nx + x2) * (nt - 1) + jnp.maximum(t2 - 1, 0)
        return jnp.where(t2 == 0, y * nx + x2, owner_ref[prompt_ref[at]])

    lane = lax.broadcasted_iota(jnp.int32, (8, group * unit_rows), 1)

    def note_source(i, line):
        return jnp.where(lane // unit_rows == i, source(i // nt, i % nt), line)

    source_line = lax.fori_loop(0, group, note_source, jnp.zeros_like(lane))
    shape = (unit_rows, group * unit_rows)
    same_row = (
        lax.broadcasted_iota(jnp.int32, shape, 0)
        == lax.broadcasted_iota(jnp.int32, shape, 1) % unit_rows
    )
    keyed = jnp.where(same_row, jnp.broadcast_to(source_line[:1], shape), -1)

    def spread_rows(i):
        spread[pl.ds(pl.multiple_of(i * unit_rows, unit_rows), unit_rows), :] = jnp.where(
            keyed == i, 1.0, 0.0
        ).astype(BF16)

    each(n_seq, spread_rows)

    is_prefix = t == 0
    mine = s * (nt - 1) + jnp.maximum(t - 1, 0)
    own_len = lax.fori_loop(
        0, n_seq, lambda i, n: n + jnp.where(owner_ref[i] == s, plen_ref[i], 0), jnp.int32(0)
    )
    live = jnp.where(is_prefix, own_len, rlen_ref[jnp.maximum(t - 1, 0), s])
    live_local = jnp.where(is_prefix, 0, live)
    prefix_count = jnp.where(is_prefix, PREFIX_ROWS, plen_ref[prompt_ref[mine]])
    slack = jnp.where(is_prefix, 0, PREFIX_ROWS)
    pair = 2 * HEAD_SIZE
    key_at = lax.broadcasted_iota(jnp.int32, (RLEN, pair), 0)
    row_at = lax.broadcasted_iota(jnp.int32, (RLEN, pair), 1) % RLEN
    row_line = lax.broadcasted_iota(jnp.int32, (1, pair), 1) % RLEN

    def columns(ref, g, p):
        at = pl.multiple_of(g * width + p * pair, HEAD_SIZE)
        return jnp.concatenate(
            [ref[:, pl.ds(at, HEAD_SIZE)], ref[:, pl.ds(at + HEAD_SIZE, HEAD_SIZE)]], axis=0
        )

    def head_columns(ref, g):
        return ref[:, pl.ds(pl.multiple_of(g * HEAD_SIZE, HEAD_SIZE), HEAD_SIZE)]

    def powers(key_rows, query_rows, allowed):
        scores = mm(key_rows, query_rows, 1, 1) * (factor * math.log2(math.e))
        return jnp.where(allowed, jnp.exp2(scores), 0.0)

    def own_part(g):
        allowed = (key_at <= row_at) & (row_at < live_local)
        key_rows, value_rows = head_columns(k, g), head_columns(v, g)
        ones = jnp.ones((8, HEAD_SIZE), BF16)
        for p in range(heads // 2):
            at = pl.ds(p * pair, pair)
            grad_rows = columns(do, g, p)
            product = grad_rows.astype(F32) * columns(o, g, p).astype(F32)
            high = product.astype(BF16)
            low = (product - high.astype(F32)).astype(BF16)
            deltas = (mm(ones, high, 1, 1) + mm(ones, low, 1, 1)).astype(BF16).astype(F32)
            delta[g, :, at] = deltas
            raised = powers(key_rows, columns(q, g, p), allowed)
            total[g, :, at] = jnp.broadcast_to(jnp.sum(raised, axis=0, keepdims=True), (8, pair))
            exps[g, :, at] = raised
            prods[g, :, at] = raised * (mm(value_rows, grad_rows, 1, 1) - deltas[:1])

    def stack(ref, g):
        at = pl.multiple_of(g * width, HEAD_SIZE)
        return jnp.concatenate(
            [ref[:, pl.ds(at + h * HEAD_SIZE, HEAD_SIZE)] for h in range(heads)], axis=0
        )

    arrived(strip, 0)

    def unit_of(x2):
        return strip.at[:, pl.ds(pl.multiple_of(x2 * HEAD_SIZE, HEAD_SIZE), HEAD_SIZE)]

    local(unit_of(x), units.at[s], 1).start()

    def send_unit(i):
        x2, y2 = (x + i) % nx, (y + i // nx) % ny
        remote(unit_of(x2), units.at[s], 1, (y2 * nx + x2, t)).start()

    each(n_seq, send_unit, 1)

    for load in loads:
        load.wait()
    own_part(0)
    each(nx // 2, own_part, 1)

    arrived(units, 1)

    def pick(i):
        picked[i] = units[source(i // nt, i % nt)]

    each(group, pick)

    def landing(ref):
        return ref.at[kind, x, pl.ds(pl.multiple_of(block * unit_rows, unit_rows), unit_rows)]

    local(picked.at[x * nt + t], landing(pre), 2).start()

    def send_picked(i):
        x2, t2 = (x + i // nt) % nx, (t + i) % nt
        remote(picked.at[x2 * nt + t2], landing(pre), 2, (y * nx + x2, t2)).start()

    each(group, send_picked, 1)
    each(nx, own_part, nx // 2)
    arrived(pre, 2)

    def prefix_part(j):
        g = (x + j) % nx
        allowed = (row_at < live) & (key_at < prefix_count) & (key_at <= row_at + slack)
        key_rows, value_rows = pre[0, g], pre[1, g]
        for p in range(heads // 2):
            at = pl.ds(p * pair, pair)
            raised = powers(key_rows, columns(q, g, p), allowed)
            row_total = total[g, :1, at] + jnp.sum(raised, axis=0, keepdims=True)
            inverse = 1.0 / jnp.where(row_line < live, row_total, 1.0)
            total[g, :, at] = jnp.broadcast_to(inverse, (8, pair))
            weights = raised * inverse
            w_low[:, at] = weights.astype(BF16)
            grad_weights = mm(value_rows, columns(do, g, p), 1, 1)
            ds_pre[g, :, at] = (weights * (grad_weights - delta[g, :1, at])).astype(BF16)
        back_out[1, g] = mm(w_low[...], stack(do, g), 1, 0).astype(BF16)
        back_out[0, g] = (mm(ds_pre[g], stack(q, g), 1, 0) * factor).astype(BF16)

        def send_back(i):
            t2 = (t + i) % nt
            unit = back_out.at[
                t2 % 2, g, pl.ds(pl.multiple_of((t2 // 2) * unit_rows, unit_rows), unit_rows)
            ]
            here = (j == 0) & (i == 0)

            @pl.when(here)
            def _():
                local(unit, back.at[x * nt + t], 3).start()

            @pl.when(jnp.logical_not(here))
            def _():
                remote(unit, back.at[x * nt + t], 3, (y * nx + g, t2)).start()

        each(nt, send_back)

    each(nx, prefix_part)

    def rest(g):
        key_rows, prefix_rows = head_columns(k, g), pre[0, g]
        for p in range(heads // 2):
            at = pl.ds(p * pair, pair)
            inverse = total[g, :1, at]
            w_low[:, at] = (exps[g, :, at] * inverse).astype(BF16)
            low = (prods[g, :, at] * inverse).astype(BF16)
            ds_low[:, at] = low
            grads = mm(ds_pre[g, :, at], prefix_rows, 0, 0) + mm(low, key_rows, 0, 0)
            grads = (grads * factor).astype(BF16)
            to = pl.multiple_of(g * width + p * pair, HEAD_SIZE)
            dq[:, pl.ds(to, HEAD_SIZE)] = grads[:RLEN]
            dq[:, pl.ds(to + HEAD_SIZE, HEAD_SIZE)] = grads[RLEN:]
        to = pl.ds(pl.multiple_of(g * HEAD_SIZE, HEAD_SIZE), HEAD_SIZE)
        dv[:, to] = mm(w_low[...], stack(do, g), 1, 0).astype(BF16)
        dk[:, to] = (mm(ds_low[...], stack(q, g), 1, 0) * factor).astype(BF16)

    each(nx, rest)
    store_query = pltpu.make_async_copy(dq, dq_hbm, out_sem.at[0])
    store_query.start()

    @pl.when(t != 0)
    def _():
        pltpu.make_async_copy(dk, dk_hbm, out_sem.at[1]).start()
        pltpu.make_async_copy(dv, dv_hbm, out_sem.at[2]).start()

    arrived(back, 3)
    gathered = back[...].reshape(group * unit_rows, HEAD_SIZE)
    sums[...] = mm(spread[...], gathered, 1, 0).astype(BF16).reshape(sums.shape)
    local(sums.at[s], parts.at[s], 4).start()

    def send_sum(i):
        x2, y2 = (x + i) % nx, (y + i // nx) % ny
        remote(sums.at[y2 * nx + x2], parts.at[s], 4, (y2 * nx + x2, t)).start()

    each(n_seq, send_sum, 1)
    arrived(parts, 4)
    for h in range(nx):
        whole = parts[h].astype(F32)
        for i in range(1, ny):
            whole += parts[i * nx + h].astype(F32)
        final[:, pl.ds(h * HEAD_SIZE, HEAD_SIZE)] = whole.astype(BF16)

    rows = pl.ds(pl.multiple_of(block * unit_rows, unit_rows), unit_rows)

    @pl.when(t == 0)
    def _():
        local(final, dk_hbm.at[rows], 5).start()

    @pl.when((t != 0) & (kind == 0))
    def _():
        remote(final, dk_hbm.at[rows], 5, (s, 0)).start()

    @pl.when(kind == 1)
    def _():
        remote(final, dv_hbm.at[rows], 6, (s, 0)).start()

    store_query.wait()
    sent(units.at[pl.ds(0, n_seq - 1)], 1)
    sent(picked.at[pl.ds(0, group - 1)], 2)
    sent(back.at[pl.ds(0, group - 1)], 3)
    sent(sums.at[pl.ds(0, n_seq - 1)], 4)

    @pl.when(t == 0)
    def _():
        sent(picked.at[pl.ds(0, (nt - 1) * nx)], 0)
        arrived(dk, 5)
        arrived(dv, 6)

    @pl.when((t != 0) & (kind == 0))
    def _():
        sent(final, 5)

    @pl.when(kind == 1)
    def _():
        sent(final, 6)

    @pl.when(t != 0)
    def _():
        pltpu.make_async_copy(dk, dk_hbm, out_sem.at[1]).wait()
        pltpu.make_async_copy(dv, dv_hbm, out_sem.at[2]).wait()


def shards(
    queries,
    key_matrix,
    value_matrix,
    attn_output,
    grad_output,
    prefix_len,
    rollout_len,
    rollout_prompt,
    prefix_owner,
):
    nt = lax.axis_size("head")
    n_seq = lax.axis_size("seq")
    nx = KEY_VALUE_HEADS
    ny = n_seq // nx
    group = nx * nt
    heads = QUERY_HEADS // nx
    width = heads * HEAD_SIZE
    unit_rows = PREFIX_ROWS // (nt // 2)
    unit = (unit_rows, HEAD_SIZE)
    anywhere = pl.BlockSpec(memory_space=pl.ANY)
    scalars = pl.BlockSpec(memory_space=pltpu.SMEM)
    wide = pltpu.VMEM(queries.shape, BF16)
    narrow = pltpu.VMEM(key_matrix.shape, BF16)
    per_head = (nx, RLEN, width)
    return pl.pallas_call(
        functools.partial(kernel, ny, nx, nt),
        out_shape=[
            jax.ShapeDtypeStruct(queries.shape, BF16),
            jax.ShapeDtypeStruct(key_matrix.shape, BF16),
            jax.ShapeDtypeStruct(value_matrix.shape, BF16),
        ],
        in_specs=[scalars] * 4 + [anywhere] * 5,
        out_specs=[anywhere] * 3,
        scratch_shapes=[
            wide,
            narrow,
            narrow,
            wide,
            wide,
            wide,
            narrow,
            narrow,
            pltpu.VMEM((unit_rows, nx * HEAD_SIZE), BF16),
            pltpu.VMEM((n_seq,) + unit, BF16),
            pltpu.VMEM((group,) + unit, BF16),
            pltpu.VMEM((2, nx, PREFIX_ROWS, HEAD_SIZE), BF16),
            pltpu.VMEM((2, nx, PREFIX_ROWS, HEAD_SIZE), BF16),
            pltpu.VMEM((group,) + unit, BF16),
            pltpu.VMEM((n_seq,) + unit, BF16),
            pltpu.VMEM((n_seq,) + unit, BF16),
            pltpu.VMEM((unit_rows, nx * HEAD_SIZE), BF16),
            pltpu.VMEM((n_seq * unit_rows, group * unit_rows), BF16),
            pltpu.VMEM(per_head, F32),
            pltpu.VMEM(per_head, F32),
            pltpu.VMEM(per_head, BF16),
            pltpu.VMEM(per_head[1:], BF16),
            pltpu.VMEM(per_head[1:], BF16),
            pltpu.VMEM((nx, 8, width), F32),
            pltpu.VMEM((nx, 8, width), F32),
            pltpu.SemaphoreType.DMA((5,)),
            pltpu.SemaphoreType.DMA((3,)),
            pltpu.SemaphoreType.DMA((7,)),
            pltpu.SemaphoreType.DMA((7,)),
        ],
        compiler_params=pltpu.CompilerParams(
            collective_id=0, has_side_effects=True, vmem_limit_bytes=VMEM_BYTES
        ),
        name="attention_backward",
    )(
        rollout_prompt.reshape(-1),
        prefix_owner,
        prefix_len,
        rollout_len.T,
        queries,
        key_matrix,
        value_matrix,
        attn_output,
        grad_output,
    )


def solution(mesh):
    rows = P(("seq", "head"), None)
    return jax.shard_map(
        shards,
        mesh=mesh,
        in_specs=(rows,) * 5 + (P(),) * 4,
        out_specs=(rows,) * 3,
        check_vma=False,
    )
```

time: 964 us -> 67.7 us (0.07)
  the two profiles are of different devices: /device:TPU:1 before, /device:TPU:16 now
where the time goes in v1:
time: 67.7 us; the launch traced here: 67.5 us
  Pallas kernels  62.9 us (93%)
  local copies, waits for them, and re-layouts  3.93 us (6%)
    pallas_call x1, Pallas kernels, shards(): pl.pallas_call(functools.partial(kernel, ny, nx, nt), out_shape=[jax.Shap...  62.9 us
    unnamed x7, local copies, waits for them, and re-layouts  3.93 us

profile of v1, /device:TPU:16, one launch (start us, length us, event | category | flops | bytes accessed | tf_op | source)
XLA Modules:
  0.0 67.5 jit_solution(4823805842296131589)
XLA Ops:
  0.6 62.9 %attention_backward.1 = (bf16[128,4096]{1,0:T(8,128)(2,1)}, bf16[128,512]{1,0:T(8,128)(2,1)}, bf16[128,512]{1,0:T(8,128)(2,1)}) custom-call(s32[480]{0:T(512)} %bitcast.3, s32[32]{0:T(128)} %owner_ref.1, s32[32]{0:T(128)} %plen_ref.1, s32[15,32]{1,0:T(8,128)} %bitcast.2, bf16[128,4096]{1,0:T(8,128)(2,1)} %q_hbm.1, bf16[128,512]{1,0:T(8,128)(2,1)} %k_hbm.1, ...), custom_call_target="tpu_custom_call" | custom-call | tf_op jit(solution)/shard_map/attention_backward/pallas_call | solution.py:400
  63.6 0.0 copy-start.1
  63.6 2.3 %copy.15 = bf16[128,4096]{1,0:T(8,128)(2,1)} copy(bf16[128,4096]{1,0:T(8,128)(2,1)} %get-tuple-element.6) | data formatting | bytes 2097152
  65.9 0.0 copy-done.1
  65.9 0.0 copy-start
  65.9 0.7 copy.16
  66.5 0.3 copy-done
  66.8 0.7 copy.17
Async XLA Ops:
  63.6 2.3 %copy-start.1 = (bf16[128,512]{1,0:T(8,128)(2,1)S(1)}, bf16[128,512]{1,0:T(8,128)(2,1)}, u32[]{:S(2)}) copy-start(bf16[128,512]{1,0:T(8,128)(2,1)} %get-tuple-element.7) | copy-start | bytes 393220
  65.9 1.0 %copy-start = (bf16[128,512]{1,0:T(8,128)(2,1)S(1)}, bf16[128,512]{1,0:T(8,128)(2,1)}, u32[]{:S(2)}) copy-start(bf16[128,512]{1,0:T(8,128)(2,1)} %get-tuple-element.8) | copy-start | bytes 393220

commit v2 on v1

--- a/solution.py
+++ b/solution.py
@@ -16,7 +16,7 @@
 MESH = pl.DeviceIdType.MESH
 F32 = jnp.float32
 BF16 = jnp.bfloat16
-VMEM_BYTES = 60 * 1024 * 1024
+VMEM_BYTES = 56 * 1024 * 1024
 
 
 def mm(a, b, da, db):
@@ -36,18 +36,16 @@
     v_hbm,
     o_hbm,
     do_hbm,
-    dq_hbm,
-    dk_hbm,
-    dv_hbm,
+    dq,
+    dk,
+    dv,
     q,
     k,
     v,
     o,
     do,
-    dq,
-    dk,
-    dv,
     strip,
+    cut,
     units,
     picked,
     pre,
@@ -57,6 +55,8 @@
     parts,
     final,
     spread,
+    partial,
+    sources,
     exps,
     prods,
     ds_pre,
@@ -65,7 +65,6 @@
     delta,
     total,
     in_sem,
-    out_sem,
     send_sem,
     recv_sem,
 ):
@@ -77,10 +76,8 @@
     factor = 1.0 / math.sqrt(HEAD_SIZE)
     s = lax.axis_index("seq")
     t = lax.axis_index("head")
-    y = s // nx
-    x = s % nx
-    kind = t % 2
-    block = t // 2
+    y, x = lax.div(s, nx), lax.rem(s, nx)
+    block, kind = lax.div(t, 2), lax.rem(t, 2)
 
     def each(count, body, start=0):
         def step(i, carry):
@@ -98,16 +95,29 @@
 
     barrier = pltpu.get_barrier_semaphore()
 
-    def greet_row(i):
-        peer = (y * nx + (x + i // nt) % nx, (t + i) % nt)
+    nz = nt // 2
+    xs = [lax.rem(x + i, nx) for i in range(nx)]
+    ys = [lax.rem(y + i, ny) for i in range(ny)]
+    zs = [lax.rem(block + i, nz) for i in range(nz)]
+    cs = [kind, 1 - kind]
+
+    def far_first(n):
+        return sorted(range(n), key=lambda i: (-min(i, n - i), i))
+
+    plane = [(i, j) for i in range(ny) for j in range(nx) if i + j > 0]
+    plane.sort(key=lambda at: -min(at[0], ny - at[0]) - min(at[1], nx - at[1]))
+    column = [(j, c) for j in far_first(nz) for c in (1, 0)]
+
+    def greet(peer):
         pl.semaphore_signal(barrier, inc=1, device_id=peer, device_id_type=MESH)
 
-    def greet_plane(i):
-        peer = (((y + 1 + i // nx) % ny) * nx + i % nx, t)
-        pl.semaphore_signal(barrier, inc=1, device_id=peer, device_id_type=MESH)
-
-    each(group, greet_row, 1)
-    each((ny - 1) * nx, greet_plane)
+    for i in far_first(nx):
+        for j, c in column:
+            if i + j + c > 0:
+                greet((y * nx + xs[i], zs[j] * 2 + cs[c]))
+    for i, j in plane:
+        if i > 0:
+            greet((ys[i] * nx + xs[j], t))
     pl.semaphore_wait(barrier, group - 1 + (ny - 1) * nx)
 
     def remote(src, dst, stage, peer):
@@ -131,26 +141,24 @@
 
     @pl.when(t == 0)
     def _():
-        local(k_hbm.at[pl.ds(0, unit_rows)], strip, 0).start()
-        remote(v_hbm.at[pl.ds(0, unit_rows)], strip, 0, (s, 1)).start()
-
-        def send_strips(i):
-            rows = pl.ds(pl.multiple_of(i * unit_rows, unit_rows), unit_rows)
-            remote(k_hbm.at[rows], strip, 0, (s, 2 * i)).start()
+        for i in far_first(nz):
+            rows = pl.ds(i * unit_rows, unit_rows)
+            if i > 0:
+                remote(k_hbm.at[rows], strip, 0, (s, 2 * i)).start()
+            else:
+                local(k_hbm.at[rows], strip, 0).start()
             remote(v_hbm.at[rows], strip, 0, (s, 2 * i + 1)).start()
 
-        each(nt // 2, send_strips, 1)
-
-    def source(x2, t2):
-        at = (y * nx + x2) * (nt - 1) + jnp.maximum(t2 - 1, 0)
-        return jnp.where(t2 == 0, y * nx + x2, owner_ref[prompt_ref[at]])
-
-    lane = lax.broadcasted_iota(jnp.int32, (8, group * unit_rows), 1)
-
-    def note_source(i, line):
-        return jnp.where(lane // unit_rows == i, source(i // nt, i % nt), line)
-
-    source_line = lax.fori_loop(0, group, note_source, jnp.zeros_like(lane))
+    for i in range(nx):
+        s2 = y * nx + xs[i]
+        sources[i * nt] = s2
+        for t2 in range(1, nt):
+            sources[i * nt + t2] = owner_ref[prompt_ref[s2 * (nt - 1) + (t2 - 1)]]
+
+    lane = lax.broadcasted_iota(jnp.int32, (8, group * unit_rows), 1) // unit_rows
+    source_line = jnp.zeros_like(lane)
+    for i in range(group):
+        source_line = jnp.where(lane == i, sources[i], source_line)
     shape = (unit_rows, group * unit_rows)
     same_row = (
         lax.broadcasted_iota(jnp.int32, shape, 0)
@@ -217,16 +225,11 @@
 
     arrived(strip, 0)
 
-    def unit_of(x2):
-        return strip.at[:, pl.ds(pl.multiple_of(x2 * HEAD_SIZE, HEAD_SIZE), HEAD_SIZE)]
-
-    local(unit_of(x), units.at[s], 1).start()
-
-    def send_unit(i):
-        x2, y2 = (x + i) % nx, (y + i // nx) % ny
-        remote(unit_of(x2), units.at[s], 1, (y2 * nx + x2, t)).start()
-
-    each(n_seq, send_unit, 1)
+    for h in range(nx):
+        cut[h] = strip[:, h * HEAD_SIZE : (h + 1) * HEAD_SIZE]
+    local(cut.at[x], units.at[s], 1).start()
+    for i, j in plane:
+        remote(cut.at[xs[j]], units.at[s], 1, (ys[i] * nx + xs[j], t)).start()
 
     for load in loads:
         load.wait()
@@ -235,26 +238,21 @@
 
     arrived(units, 1)
 
-    def pick(i):
-        picked[i] = units[source(i // nt, i % nt)]
-
-    each(group, pick)
-
-    def landing(ref):
-        return ref.at[kind, x, pl.ds(pl.multiple_of(block * unit_rows, unit_rows), unit_rows)]
-
-    local(picked.at[x * nt + t], landing(pre), 2).start()
-
-    def send_picked(i):
-        x2, t2 = (x + i // nt) % nx, (t + i) % nt
-        remote(picked.at[x2 * nt + t2], landing(pre), 2, (y * nx + x2, t2)).start()
-
-    each(group, send_picked, 1)
+    landing = pre.at[kind, x, pl.ds(pl.multiple_of(block * unit_rows, unit_rows), unit_rows)]
+    for i in far_first(nx):
+        for t2 in range(nt):
+            picked[i * nt + t2] = units[sources[i * nt + t2]]
+        for j, c in column:
+            t2 = zs[j] * 2 + cs[c]
+            if i + j + c == 0:
+                local(picked.at[t], landing, 7).start()
+            else:
+                remote(picked.at[i * nt + t2], landing, 7 + i, (y * nx + xs[i], t2)).start()
     each(nx, own_part, nx // 2)
-    arrived(pre, 2)
-
-    def prefix_part(j):
-        g = (x + j) % nx
+
+    def prefix_part(i):
+        g = xs[(nx - i) % nx]
+        arrived(pre.at[:, g], 7 + i)
         allowed = (row_at < live) & (key_at < prefix_count) & (key_at <= row_at + slack)
         key_rows, value_rows = pre[0, g], pre[1, g]
         for p in range(heads // 2):
@@ -270,24 +268,18 @@
         back_out[1, g] = mm(w_low[...], stack(do, g), 1, 0).astype(BF16)
         back_out[0, g] = (mm(ds_pre[g], stack(q, g), 1, 0) * factor).astype(BF16)
 
-        def send_back(i):
-            t2 = (t + i) % nt
+        for j, c in column:
+            t2 = zs[j] * 2 + cs[c]
             unit = back_out.at[
-                t2 % 2, g, pl.ds(pl.multiple_of((t2 // 2) * unit_rows, unit_rows), unit_rows)
+                cs[c], g, pl.ds(pl.multiple_of(zs[j] * unit_rows, unit_rows), unit_rows)
             ]
-            here = (j == 0) & (i == 0)
-
-            @pl.when(here)
-            def _():
-                local(unit, back.at[x * nt + t], 3).start()
-
-            @pl.when(jnp.logical_not(here))
-            def _():
-                remote(unit, back.at[x * nt + t], 3, (y * nx + g, t2)).start()
-
-        each(nt, send_back)
-
-    each(nx, prefix_part)
+            if i + j + c == 0:
+                local(unit, back.at[t], 7 + nx).start()
+            else:
+                remote(unit, back.at[i * nt + t], 7 + nx + i, (y * nx + g, t2)).start()
+
+    for i in far_first(nx):
+        prefix_part(i)
 
     def rest(g):
         key_rows, prefix_rows = head_columns(k, g), pre[0, g]
@@ -303,28 +295,30 @@
             dq[:, pl.ds(to, HEAD_SIZE)] = grads[:RLEN]
             dq[:, pl.ds(to + HEAD_SIZE, HEAD_SIZE)] = grads[RLEN:]
         to = pl.ds(pl.multiple_of(g * HEAD_SIZE, HEAD_SIZE), HEAD_SIZE)
-        dv[:, to] = mm(w_low[...], stack(do, g), 1, 0).astype(BF16)
-        dk[:, to] = (mm(ds_low[...], stack(q, g), 1, 0) * factor).astype(BF16)
+
+        @pl.when(t != 0)
+        def _():
+            dv[:, to] = mm(w_low[...], stack(do, g), 1, 0).astype(BF16)
+            dk[:, to] = (mm(ds_low[...], stack(q, g), 1, 0) * factor).astype(BF16)
 
     each(nx, rest)
-    store_query = pltpu.make_async_copy(dq, dq_hbm, out_sem.at[0])
-    store_query.start()
-
-    @pl.when(t != 0)
-    def _():
-        pltpu.make_async_copy(dk, dk_hbm, out_sem.at[1]).start()
-        pltpu.make_async_copy(dv, dv_hbm, out_sem.at[2]).start()
-
-    arrived(back, 3)
-    gathered = back[...].reshape(group * unit_rows, HEAD_SIZE)
-    sums[...] = mm(spread[...], gathered, 1, 0).astype(BF16).reshape(sums.shape)
+
+    depth = nt * unit_rows
+    for n, i in enumerate(far_first(nx)):
+        arrived(back.at[pl.ds(i * nt, nt)], 7 + nx + i)
+        gathered = back[pl.ds(i * nt, nt)].reshape(depth, HEAD_SIZE)
+        added = mm(spread[:, pl.ds(i * depth, depth)], gathered, 1, 0)
+        if n > 0:
+            added += partial[...]
+        if n < nx - 1:
+            partial[...] = added
+        else:
+            sums[...] = added.astype(BF16).reshape(sums.shape)
     local(sums.at[s], parts.at[s], 4).start()
 
-    def send_sum(i):
-        x2, y2 = (x + i) % nx, (y + i // nx) % ny
-        remote(sums.at[y2 * nx + x2], parts.at[s], 4, (y2 * nx + x2, t)).start()
-
-    each(n_seq, send_sum, 1)
+    for i, j in plane:
+        s2 = ys[i] * nx + xs[j]
+        remote(sums.at[s2], parts.at[s], 4, (s2, t)).start()
     arrived(parts, 4)
     for h in range(nx):
         whole = parts[h].astype(F32)
@@ -336,20 +330,21 @@
 
     @pl.when(t == 0)
     def _():
-        local(final, dk_hbm.at[rows], 5).start()
+        local(final, dk.at[rows], 5).start()
 
     @pl.when((t != 0) & (kind == 0))
     def _():
-        remote(final, dk_hbm.at[rows], 5, (s, 0)).start()
+        remote(final, dk.at[rows], 5, (s, 0)).start()
 
     @pl.when(kind == 1)
     def _():
-        remote(final, dv_hbm.at[rows], 6, (s, 0)).start()
-
-    store_query.wait()
+        remote(final, dv.at[rows], 6, (s, 0)).start()
+
     sent(units.at[pl.ds(0, n_seq - 1)], 1)
-    sent(picked.at[pl.ds(0, group - 1)], 2)
-    sent(back.at[pl.ds(0, group - 1)], 3)
+    for i in range(nx):
+        count = nt if i > 0 else nt - 1
+        sent(picked.at[pl.ds(0, count)], 7 + i)
+        sent(back.at[pl.ds(0, count)], 7 + nx + i)
     sent(sums.at[pl.ds(0, n_seq - 1)], 4)
 
     @pl.when(t == 0)
@@ -365,11 +360,6 @@
     @pl.when(kind == 1)
     def _():
         sent(final, 6)
-
-    @pl.when(t != 0)
-    def _():
-        pltpu.make_async_copy(dk, dk_hbm, out_sem.at[1]).wait()
-        pltpu.make_async_copy(dv, dv_hbm, out_sem.at[2]).wait()
 
 
 def shards(
@@ -394,28 +384,23 @@
     unit = (unit_rows, HEAD_SIZE)
     anywhere = pl.BlockSpec(memory_space=pl.ANY)
     scalars = pl.BlockSpec(memory_space=pltpu.SMEM)
+    resident = pl.BlockSpec(memory_space=pltpu.VMEM)
     wide = pltpu.VMEM(queries.shape, BF16)
     narrow = pltpu.VMEM(key_matrix.shape, BF16)
     per_head = (nx, RLEN, width)
     return pl.pallas_call(
         functools.partial(kernel, ny, nx, nt),
-        out_shape=[
-            jax.ShapeDtypeStruct(queries.shape, BF16),
-            jax.ShapeDtypeStruct(key_matrix.shape, BF16),
-            jax.ShapeDtypeStruct(value_matrix.shape, BF16),
-        ],
+        out_shape=[wide, narrow, narrow],
         in_specs=[scalars] * 4 + [anywhere] * 5,
-        out_specs=[anywhere] * 3,
+        out_specs=[resident] * 3,
         scratch_shapes=[
             wide,
             narrow,
             narrow,
             wide,
             wide,
-            wide,
-            narrow,
-            narrow,
             pltpu.VMEM((unit_rows, nx * HEAD_SIZE), BF16),
+            pltpu.VMEM((nx,) + unit, BF16),
             pltpu.VMEM((n_seq,) + unit, BF16),
             pltpu.VMEM((group,) + unit, BF16),
             pltpu.VMEM((2, nx, PREFIX_ROWS, HEAD_SIZE), BF16),
@@ -425,6 +410,8 @@
             pltpu.VMEM((n_seq,) + unit, BF16),
             pltpu.VMEM((unit_rows, nx * HEAD_SIZE), BF16),
             pltpu.VMEM((n_seq * unit_rows, group * unit_rows), BF16),
+            pltpu.VMEM((n_seq * unit_rows, HEAD_SIZE), F32),
+            pltpu.SMEM((group,), jnp.int32),
             pltpu.VMEM(per_head, F32),
             pltpu.VMEM(per_head, F32),
             pltpu.VMEM(per_head, BF16),
@@ -433,9 +420,8 @@
             pltpu.VMEM((nx, 8, width), F32),
             pltpu.VMEM((nx, 8, width), F32),
             pltpu.SemaphoreType.DMA((5,)),
-            pltpu.SemaphoreType.DMA((3,)),
-            pltpu.SemaphoreType.DMA((7,)),
-            pltpu.SemaphoreType.DMA((7,)),
+            pltpu.SemaphoreType.DMA((7 + 2 * nx,)),
+            pltpu.SemaphoreType.DMA((7 + 2 * nx,)),
         ],
         compiler_params=pltpu.CompilerParams(
             collective_id=0, has_side_effects=True, vmem_limit_bytes=VMEM_BYTES

time: 67.7 us -> 56.5 us (0.83)
  the two profiles are of different devices: /device:TPU:16 before, /device:TPU:8 now
where the time goes in v2:
time: 56.5 us; the launch traced here: 56.3 us
  Pallas kernels  53.3 us (94%)
  local copies, waits for them, and re-layouts  2.28 us (4%)
  between operations  0.64 us (1%)
    pallas_call x1, Pallas kernels, shards(): pl.pallas_call(functools.partial(kernel, ny, nx, nt), out_shape=[wide, na...  53.3 us
    unnamed x3, local copies, waits for them, and re-layouts  2.28 us

profile of v2, /device:TPU:8, one launch (start us, length us, event | category | flops | bytes accessed | tf_op | source)
XLA Modules:
  0.0 56.3 jit_solution(4358013849186892555)
XLA Ops:
  0.6 53.3 %attention_backward.1 = (bf16[128,4096]{1,0:T(8,128)(2,1)S(1)}, bf16[128,512]{1,0:T(8,128)(2,1)S(1)}, bf16[128,512]{1,0:T(8,128)(2,1)S(1)}) custom-call(s32[480]{0:T(512)} %bitcast.3, s32[32]{0:T(128)} %owner_ref.1, s32[32]{0:T(128)} %plen_ref.1, s32[15,32]{1,0:T(8,128)} %bitcast.2, bf16[128,4096]{1,0:T(8,128)(2,1)} %q_hbm.1, bf16[128,512]{1,0:T(8,128)(2,1)} %k_hbm.1, ...), custom_call_target="tpu_custom_call" | custom-call | tf_op jit(solution)/shard_map/attention_backward/pallas_call | solution.py:391
  54.0 1.0 %copy.15 = bf16[128,4096]{1,0:T(8,128)(2,1)} copy(bf16[128,4096]{1,0:T(8,128)(2,1)S(1)} %get-tuple-element.3) | data formatting | bytes 2097152
  55.0 0.7 %copy.16 = bf16[128,512]{1,0:T(8,128)(2,1)} copy(bf16[128,512]{1,0:T(8,128)(2,1)S(1)} %get-tuple-element.4) | data formatting | bytes 262144
  55.6 0.7 %copy.17 = bf16[128,512]{1,0:T(8,128)(2,1)} copy(bf16[128,512]{1,0:T(8,128)(2,1)S(1)} %get-tuple-element.5) | data formatting | bytes 262144

commit v3 on v2

--- a/solution.py
+++ b/solution.py
@@ -64,6 +64,7 @@
     ds_low,
     delta,
     total,
+    known,
     in_sem,
     send_sem,
     recv_sem,
@@ -108,17 +109,17 @@
     plane.sort(key=lambda at: -min(at[0], ny - at[0]) - min(at[1], nx - at[1]))
     column = [(j, c) for j in far_first(nz) for c in (1, 0)]
 
-    def greet(peer):
-        pl.semaphore_signal(barrier, inc=1, device_id=peer, device_id_type=MESH)
-
-    for i in far_first(nx):
-        for j, c in column:
-            if i + j + c > 0:
-                greet((y * nx + xs[i], zs[j] * 2 + cs[c]))
-    for i, j in plane:
-        if i > 0:
-            greet((ys[i] * nx + xs[j], t))
-    pl.semaphore_wait(barrier, group - 1 + (ny - 1) * nx)
+    def greet(semaphore, peer):
+        pl.semaphore_signal(semaphore, inc=1, device_id=peer, device_id_type=MESH)
+
+    line_y = [(ys[i] * nx + x, t) for i in far_first(ny) if i > 0]
+    line_x = [(y * nx + xs[i], t) for i in far_first(nx) if i > 0]
+    line_t = [(s, zs[j] * 2 + cs[c]) for j, c in column if j + c > 0]
+    for peer in line_t + line_y + line_x:
+        greet(barrier, peer)
+    pl.semaphore_wait(barrier, len(line_t) + len(line_y) + len(line_x))
+    for peer in line_y + line_t:
+        greet(known, peer)
 
     def remote(src, dst, stage, peer):
         return pltpu.make_async_remote_copy(
@@ -223,6 +224,7 @@
             [ref[:, pl.ds(at + h * HEAD_SIZE, HEAD_SIZE)] for h in range(heads)], axis=0
         )
 
+    pl.semaphore_wait(known, len(line_y) + len(line_t))
     arrived(strip, 0)
 
     for h in range(nx):
@@ -419,6 +421,7 @@
             pltpu.VMEM(per_head[1:], BF16),
             pltpu.VMEM((nx, 8, width), F32),
             pltpu.VMEM((nx, 8, width), F32),
+            pltpu.SemaphoreType.REGULAR,
             pltpu.SemaphoreType.DMA((5,)),
             pltpu.SemaphoreType.DMA((7 + 2 * nx,)),
             pltpu.SemaphoreType.DMA((7 + 2 * nx,)),

time: 56.5 us -> 55.1 us (0.975)
  Pallas kernels: 53.3 us -> 52 us
    pallas_call x1, Pallas kernels: 53.3 us -> 52 us  [shards(): pl.pallas_call(functools.partial(kernel, ny, nx, nt), out_shape=[wide, na...]
where the time goes in v3:
time: 55.1 us; the launch traced here: 54.9 us
  Pallas kernels  52 us (94%)
  local copies, waits for them, and re-layouts  2.28 us (4%)
  between operations  0.64 us (1%)
    pallas_call x1, Pallas kernels, shards(): pl.pallas_call(functools.partial(kernel, ny, nx, nt), out_shape=[wide, na...  52 us
    unnamed x3, local copies, waits for them, and re-layouts  2.28 us

profile of v3, /device:TPU:8, one launch (start us, length us, event | category | flops | bytes accessed | tf_op | source)
XLA Modules:
  0.0 54.9 jit_solution(15316902984889650387)
XLA Ops:
  0.6 52.0 %attention_backward.1 = (bf16[128,4096]{1,0:T(8,128)(2,1)S(1)}, bf16[128,512]{1,0:T(8,128)(2,1)S(1)}, bf16[128,512]{1,0:T(8,128)(2,1)S(1)}) custom-call(s32[480]{0:T(512)} %bitcast.3, s32[32]{0:T(128)} %owner_ref.1, s32[32]{0:T(128)} %plen_ref.1, s32[15,32]{1,0:T(8,128)} %bitcast.2, bf16[128,4096]{1,0:T(8,128)(2,1)} %q_hbm.1, bf16[128,512]{1,0:T(8,128)(2,1)} %k_hbm.1, ...), custom_call_target="tpu_custom_call" | custom-call | tf_op jit(solution)/shard_map/attention_backward/pallas_call | solution.py:393
  52.7 1.0 %copy.15 = bf16[128,4096]{1,0:T(8,128)(2,1)} copy(bf16[128,4096]{1,0:T(8,128)(2,1)S(1)} %get-tuple-element.3) | data formatting | bytes 2097152
  53.6 0.7 %copy.16 = bf16[128,512]{1,0:T(8,128)(2,1)} copy(bf16[128,512]{1,0:T(8,128)(2,1)S(1)} %get-tuple-element.4) | data formatting | bytes 262144
  54.3 0.7 %copy.17 = bf16[128,512]{1,0:T(8,128)(2,1)} copy(bf16[128,512]{1,0:T(8,128)(2,1)S(1)} %get-tuple-element.5) | data formatting | bytes 262144

commit v4 on v3

--- a/solution.py
+++ b/solution.py
@@ -142,13 +142,15 @@
 
     @pl.when(t == 0)
     def _():
+        loads[1].wait()
+        loads[2].wait()
         for i in far_first(nz):
             rows = pl.ds(i * unit_rows, unit_rows)
             if i > 0:
-                remote(k_hbm.at[rows], strip, 0, (s, 2 * i)).start()
+                remote(k.at[rows], strip, 0, (s, 2 * i)).start()
             else:
-                local(k_hbm.at[rows], strip, 0).start()
-            remote(v_hbm.at[rows], strip, 0, (s, 2 * i + 1)).start()
+                local(k.at[rows], strip, 0).start()
+            remote(v.at[rows], strip, 0, (s, 2 * i + 1)).start()
 
     for i in range(nx):
         s2 = y * nx + xs[i]
@@ -233,8 +235,13 @@
     for i, j in plane:
         remote(cut.at[xs[j]], units.at[s], 1, (ys[i] * nx + xs[j], t)).start()
 
-    for load in loads:
-        load.wait()
+    @pl.when(t != 0)
+    def _():
+        loads[1].wait()
+        loads[2].wait()
+
+    for i in (0, 3, 4):
+        loads[i].wait()
     own_part(0)
     each(nx // 2, own_part, 1)
 
@@ -362,6 +369,19 @@
     @pl.when(kind == 1)
     def _():
         sent(final, 6)
+
+
+def hand_over(dq, dk, dv, dq_out, dk_out, dv_out, sem):
+    rows = dq.shape[0] // 4
+    pairs = [(dq.at[pl.ds(i * rows, rows)], dq_out.at[pl.ds(i * rows, rows)]) for i in range(4)]
+    copies = [
+        pltpu.make_async_copy(a, b, sem.at[i])
+        for i, (a, b) in enumerate(pairs + [(dk, dk_out), (dv, dv_out)])
+    ]
+    for copy in copies:
+        copy.start()
+    for copy in copies:
+        copy.wait()
 
 
 def shards(
@@ -390,7 +410,7 @@
     wide = pltpu.VMEM(queries.shape, BF16)
     narrow = pltpu.VMEM(key_matrix.shape, BF16)
     per_head = (nx, RLEN, width)
-    return pl.pallas_call(
+    grads = pl.pallas_call(
         functools.partial(kernel, ny, nx, nt),
         out_shape=[wide, narrow, narrow],
         in_specs=[scalars] * 4 + [anywhere] * 5,
@@ -441,6 +461,16 @@
         attn_output,
         grad_output,
     )
+    grads = [pltpu.with_memory_space_constraint(grad, pltpu.VMEM) for grad in grads]
+    return pl.pallas_call(
+        hand_over,
+        out_shape=[jax.ShapeDtypeStruct(grad.shape, BF16) for grad in grads],
+        in_specs=[resident] * 3,
+        out_specs=[anywhere] * 3,
+        scratch_shapes=[pltpu.SemaphoreType.DMA((6,))],
+        compiler_params=pltpu.CompilerParams(vmem_limit_bytes=VMEM_BYTES),
+        name="hand_over",
+    )(*grads)
 
 
 def solution(mesh):

time: 55.1 us -> 53.6 us (0.973)
  local copies, waits for them, and re-layouts: 2.28 us -> 0 us
  Pallas kernels: 52 us -> 52.8 us
    unnamed x3 -> x0, local copies, waits for them, and re-layouts: 2.28 us -> none
    pallas_call x0 -> x1, Pallas kernels: none -> 1.1 us  [shards(): pl.pallas_call(hand_over, out_shape=[jax.ShapeDtypeStruct(grad.shape, BF1...]
where the time goes in v4:
time: 53.6 us; the launch traced here: 53.5 us
  Pallas kernels  52.8 us (99%)
  between operations  0.64 us (1%)
    pallas_call x1, Pallas kernels, shards(): pl.pallas_call(functools.partial(kernel, ny, nx, nt), out_shape=[wide, na...  51.7 us
    pallas_call x1, Pallas kernels, shards(): pl.pallas_call(hand_over, out_shape=[jax.ShapeDtypeStruct(grad.shape, BF1...  1.1 us

profile of v4, /device:TPU:8, one launch (start us, length us, event | category | flops | bytes accessed | tf_op | source)
XLA Modules:
  0.0 53.5 jit_solution(5435800605622663976)
XLA Ops:
  0.6 51.7 %attention_backward.1 = (bf16[128,4096]{1,0:T(8,128)(2,1)S(1)}, bf16[128,512]{1,0:T(8,128)(2,1)S(1)}, bf16[128,512]{1,0:T(8,128)(2,1)S(1)}) custom-call(s32[480]{0:T(512)} %bitcast.3, s32[32]{0:T(128)} %owner_ref.1, s32[32]{0:T(128)} %plen_ref.1, s32[15,32]{1,0:T(8,128)} %bitcast.2, bf16[128,4096]{1,0:T(8,128)(2,1)} %q_hbm.1, bf16[128,512]{1,0:T(8,128)(2,1)} %k_hbm.1, ...), custom_call_target="tpu_custom_call" | custom-call | tf_op jit(solution)/shard_map/attention_backward/pallas_call | solution.py:413
  52.4 1.1 %hand_over.1 = (bf16[128,4096]{1,0:T(8,128)(2,1)}, bf16[128,512]{1,0:T(8,128)(2,1)}, bf16[128,512]{1,0:T(8,128)(2,1)}) custom-call(bf16[128,4096]{1,0:T(8,128)(2,1)S(1)} %get-tuple-element.6.dq, bf16[128,512]{1,0:T(8,128)(2,1)S(1)} %get-tuple-element.7.dk, bf16[128,512]{1,0:T(8,128)(2,1)S(1)} %get-tuple-element.8.dv), custom_call_target="tpu_custom_call" | custom-call | tf_op jit(solution)/shard_map/hand_over/pallas_call | solution.py:465

commit v5 on v4

--- a/solution.py
+++ b/solution.py
@@ -91,9 +91,6 @@
         pltpu.make_async_copy(a, b, in_sem.at[i])
         for i, (a, b) in enumerate(((q_hbm, q), (k_hbm, k), (v_hbm, v), (do_hbm, do), (o_hbm, o)))
     ]
-    for load in loads:
-        load.start()
-
     barrier = pltpu.get_barrier_semaphore()
 
     nz = nt // 2
@@ -105,6 +102,7 @@
     def far_first(n):
         return sorted(range(n), key=lambda i: (-min(i, n - i), i))
 
+    turns = [(n + 1) % nx for n in range(nx)]
     plane = [(i, j) for i in range(ny) for j in range(nx) if i + j > 0]
     plane.sort(key=lambda at: -min(at[0], ny - at[0]) - min(at[1], nx - at[1]))
     column = [(j, c) for j in far_first(nz) for c in (1, 0)]
@@ -115,12 +113,14 @@
     line_y = [(ys[i] * nx + x, t) for i in far_first(ny) if i > 0]
     line_x = [(y * nx + xs[i], t) for i in far_first(nx) if i > 0]
     line_t = [(s, zs[j] * 2 + cs[c]) for j, c in column if j + c > 0]
-    for peer in line_t + line_y + line_x:
+    pl.when(t != 0)(functools.partial(greet, barrier, (s, 0)))
+    for peer in line_y + line_x:
         greet(barrier, peer)
+    for peer in line_t:
+        pl.when(peer[1] != 0)(functools.partial(greet, barrier, peer))
+    for load in loads:
+        load.start()
     pl.semaphore_wait(barrier, len(line_t) + len(line_y) + len(line_x))
-    for peer in line_y + line_t:
-        greet(known, peer)
-
     def remote(src, dst, stage, peer):
         return pltpu.make_async_remote_copy(
             src_ref=src,
@@ -151,6 +151,9 @@
             else:
                 local(k.at[rows], strip, 0).start()
             remote(v.at[rows], strip, 0, (s, 2 * i + 1)).start()
+
+    for peer in line_y + line_t:
+        greet(known, peer)
 
     for i in range(nx):
         s2 = y * nx + xs[i]
@@ -248,20 +251,28 @@
     arrived(units, 1)
 
     landing = pre.at[kind, x, pl.ds(pl.multiple_of(block * unit_rows, unit_rows), unit_rows)]
-    for i in far_first(nx):
+    for i in turns:
         for t2 in range(nt):
             picked[i * nt + t2] = units[sources[i * nt + t2]]
         for j, c in column:
             t2 = zs[j] * 2 + cs[c]
             if i + j + c == 0:
-                local(picked.at[t], landing, 7).start()
+                pl.when(t != 0)(local(picked.at[t], landing, 7).start)
             else:
-                remote(picked.at[i * nt + t2], landing, 7 + i, (y * nx + xs[i], t2)).start()
+                copy = remote(picked.at[i * nt + t2], landing, 7 + i, (y * nx + xs[i], t2))
+                pl.when(t2 != 0)(copy.start)
     each(nx, own_part, nx // 2)
+
+    @pl.when(t == 0)
+    def _():
+        for h in range(nx):
+            pre[0, h] = k[:, h * HEAD_SIZE : (h + 1) * HEAD_SIZE]
+            pre[1, h] = v[:, h * HEAD_SIZE : (h + 1) * HEAD_SIZE]
+
 
     def prefix_part(i):
         g = xs[(nx - i) % nx]
-        arrived(pre.at[:, g], 7 + i)
+        pl.when(t != 0)(functools.partial(arrived, pre.at[:, g], 7 + i))
         allowed = (row_at < live) & (key_at < prefix_count) & (key_at <= row_at + slack)
         key_rows, value_rows = pre[0, g], pre[1, g]
         for p in range(heads // 2):
@@ -287,7 +298,7 @@
             else:
                 remote(unit, back.at[i * nt + t], 7 + nx + i, (y * nx + g, t2)).start()
 
-    for i in far_first(nx):
+    for i in turns:
         prefix_part(i)
 
     def rest(g):
@@ -313,7 +324,7 @@
     each(nx, rest)
 
     depth = nt * unit_rows
-    for n, i in enumerate(far_first(nx)):
+    for n, i in enumerate(turns):
         arrived(back.at[pl.ds(i * nt, nt)], 7 + nx + i)
         gathered = back[pl.ds(i * nt, nt)].reshape(depth, HEAD_SIZE)
         added = mm(spread[:, pl.ds(i * depth, depth)], gathered, 1, 0)
@@ -352,7 +363,11 @@
     sent(units.at[pl.ds(0, n_seq - 1)], 1)
     for i in range(nx):
         count = nt if i > 0 else nt - 1
-        sent(picked.at[pl.ds(0, count)], 7 + i)
+        if i > 0:
+            sent(picked.at[pl.ds(0, nt - 1)], 7 + i)
+        else:
+            pl.when(t == 0)(functools.partial(sent, picked.at[pl.ds(0, nt - 1)], 7))
+            pl.when(t != 0)(functools.partial(sent, picked.at[pl.ds(0, nt - 2)], 7))
         sent(back.at[pl.ds(0, count)], 7 + nx + i)
     sent(sums.at[pl.ds(0, n_seq - 1)], 4)
 

time: 53.6 us -> 53 us (0.989)
  Pallas kernels: 52.8 us -> 52.1 us
    pallas_call x1, Pallas kernels: 51.7 us -> 51 us  [shards(): pl.pallas_call(functools.partial(kernel, ny, nx, nt), out_shape=[wide, na...]
where the time goes in v5:
time: 53 us; the launch traced here: 52.8 us
  Pallas kernels  52.1 us (98%)
  between operations  0.64 us (1%)
    pallas_call x1, Pallas kernels, shards(): pl.pallas_call(functools.partial(kernel, ny, nx, nt), out_shape=[wide, na...  51 us
    pallas_call x1, Pallas kernels, shards(): pl.pallas_call(hand_over, out_shape=[jax.ShapeDtypeStruct(grad.shape, BF1...  1.1 us

profile of v5, /device:TPU:8, one launch (start us, length us, event | category | flops | bytes accessed | tf_op | source)
XLA Modules:
  0.0 52.8 jit_solution(17065822935288295531)
XLA Ops:
  0.6 51.0 %attention_backward.1 = (bf16[128,4096]{1,0:T(8,128)(2,1)S(1)}, bf16[128,512]{1,0:T(8,128)(2,1)S(1)}, bf16[128,512]{1,0:T(8,128)(2,1)S(1)}) custom-call(s32[480]{0:T(512)} %bitcast.3, s32[32]{0:T(128)} %owner_ref.1, s32[32]{0:T(128)} %plen_ref.1, s32[15,32]{1,0:T(8,128)} %bitcast.2, bf16[128,4096]{1,0:T(8,128)(2,1)} %q_hbm.1, bf16[128,512]{1,0:T(8,128)(2,1)} %k_hbm.1, ...), custom_call_target="tpu_custom_call" | custom-call | tf_op jit(solution)/shard_map/attention_backward/pallas_call | solution.py:428
  51.7 1.1 %hand_over.1 = (bf16[128,4096]{1,0:T(8,128)(2,1)}, bf16[128,512]{1,0:T(8,128)(2,1)}, bf16[128,512]{1,0:T(8,128)(2,1)}) custom-call(bf16[128,4096]{1,0:T(8,128)(2,1)S(1)} %get-tuple-element.6.dq, bf16[128,512]{1,0:T(8,128)(2,1)S(1)} %get-tuple-element.7.dk, bf16[128,512]{1,0:T(8,128)(2,1)S(1)} %get-tuple-element.8.dv), custom_call_target="tpu_custom_call" | custom-call | tf_op jit(solution)/shard_map/hand_over/pallas_call | solution.py:480

commit v6 on v5

--- a/solution.py
+++ b/solution.py
@@ -270,6 +270,9 @@
             pre[1, h] = v[:, h * HEAD_SIZE : (h + 1) * HEAD_SIZE]
 
 
+    for i in range(nx):
+        back[i * nt] = jnp.zeros((unit_rows, HEAD_SIZE), BF16)
+
     def prefix_part(i):
         g = xs[(nx - i) % nx]
         pl.when(t != 0)(functools.partial(arrived, pre.at[:, g], 7 + i))
@@ -294,9 +297,10 @@
                 cs[c], g, pl.ds(pl.multiple_of(zs[j] * unit_rows, unit_rows), unit_rows)
             ]
             if i + j + c == 0:
-                local(unit, back.at[t], 7 + nx).start()
+                copy = local(unit, back.at[t], 7 + nx)
             else:
-                remote(unit, back.at[i * nt + t], 7 + nx + i, (y * nx + g, t2)).start()
+                copy = remote(unit, back.at[i * nt + t], 7 + nx + i, (y * nx + g, t2))
+            pl.when(t != 0)(copy.start)
 
     for i in turns:
         prefix_part(i)
@@ -325,7 +329,7 @@
 
     depth = nt * unit_rows
     for n, i in enumerate(turns):
-        arrived(back.at[pl.ds(i * nt, nt)], 7 + nx + i)
+        arrived(back.at[pl.ds(i * nt + 1, nt - 1)], 7 + nx + i)
         gathered = back[pl.ds(i * nt, nt)].reshape(depth, HEAD_SIZE)
         added = mm(spread[:, pl.ds(i * depth, depth)], gathered, 1, 0)
         if n > 0:
@@ -368,7 +372,7 @@
         else:
             pl.when(t == 0)(functools.partial(sent, picked.at[pl.ds(0, nt - 1)], 7))
             pl.when(t != 0)(functools.partial(sent, picked.at[pl.ds(0, nt - 2)], 7))
-        sent(back.at[pl.ds(0, count)], 7 + nx + i)
+        pl.when(t != 0)(functools.partial(sent, back.at[pl.ds(0, count)], 7 + nx + i))
     sent(sums.at[pl.ds(0, n_seq - 1)], 4)
 
     @pl.when(t == 0)
@@ -376,6 +380,10 @@
         sent(picked.at[pl.ds(0, (nt - 1) * nx)], 0)
         arrived(dk, 5)
         arrived(dv, 6)
+        for h in range(nx):
+            at = pl.ds(h * HEAD_SIZE, HEAD_SIZE)
+            dk[:, at] = (dk[:, at].astype(F32) + back_out[0, h].astype(F32)).astype(BF16)
+            dv[:, at] = (dv[:, at].astype(F32) + back_out[1, h].astype(F32)).astype(BF16)
 
     @pl.when((t != 0) & (kind == 0))
     def _():

time: 53 us -> 53 us (level)
  no operation moved by 1% of the time
where the time goes in v6:
time: 53 us; the launch traced here: 52.8 us
  Pallas kernels  52.2 us (98%)
  between operations  0.64 us (1%)
    pallas_call x1, Pallas kernels, shards(): pl.pallas_call(functools.partial(kernel, ny, nx, nt), out_shape=[wide, na...  51.1 us
    pallas_call x1, Pallas kernels, shards(): pl.pallas_call(hand_over, out_shape=[jax.ShapeDtypeStruct(grad.shape, BF1...  1.1 us

profile of v6, /device:TPU:8, one launch (start us, length us, event | category | flops | bytes accessed | tf_op | source)
XLA Modules:
  0.0 52.8 jit_solution(10849418618397565815)
XLA Ops:
  0.6 51.1 %attention_backward.1 = (bf16[128,4096]{1,0:T(8,128)(2,1)S(1)}, bf16[128,512]{1,0:T(8,128)(2,1)S(1)}, bf16[128,512]{1,0:T(8,128)(2,1)S(1)}) custom-call(s32[480]{0:T(512)} %bitcast.3, s32[32]{0:T(128)} %owner_ref.1, s32[32]{0:T(128)} %plen_ref.1, s32[15,32]{1,0:T(8,128)} %bitcast.2, bf16[128,4096]{1,0:T(8,128)(2,1)} %q_hbm.1, bf16[128,512]{1,0:T(8,128)(2,1)} %k_hbm.1, ...), custom_call_target="tpu_custom_call" | custom-call | tf_op jit(solution)/shard_map/attention_backward/pallas_call | solution.py:436
  51.7 1.1 %hand_over.1 = (bf16[128,4096]{1,0:T(8,128)(2,1)}, bf16[128,512]{1,0:T(8,128)(2,1)}, bf16[128,512]{1,0:T(8,128)(2,1)}) custom-call(bf16[128,4096]{1,0:T(8,128)(2,1)S(1)} %get-tuple-element.6.dq, bf16[128,512]{1,0:T(8,128)(2,1)S(1)} %get-tuple-element.7.dk, bf16[128,512]{1,0:T(8,128)(2,1)S(1)} %get-tuple-element.8.dv), custom_call_target="tpu_custom_call" | custom-call | tf_op jit(solution)/shard_map/hand_over/pallas_call | solution.py:488
